TPU v7x, 768 devices: a whole 4x8x12 slice. The times are simulated.
768 devices in a mesh: pop: 48 (over y, z_lo), col: 16 (over z_hi, x, core).
Axes of the slice: x: 4, y: 8, z: 12 (z_hi: 2, z_lo: 6; z = z_hi * 6 + z_lo), core: 2. Of those that a mesh axis runs over, the one named last changes fastest.
Arguments:
- weight: float32 [2304, 16384], P('pop', 'col'), may hold values from -3 to 3
- row_factors: bfloat16 [2304, 4608], P(None, 'pop'), may hold values from -6 to 6
- col_factors: bfloat16 [4608, 16384], P('pop', 'col'), may hold values from -6 to 6
- fitness_ranks: int32 [4608], P('pop'), may hold values from 0 to 4607, each once
Outputs:
- new_weight: float32 [2304, 16384], P('pop', 'col')
Inputs may be any that keep to these rules, and one draw needn't show every extreme that they name: fitness_ranks holds each of 0 to 4607 exactly once.
All inputs are finite; a program needn't handle non-finite values.
Results may differ from a plain program's by a relative error of at most 0.0026.
Values may be sent and summed in bfloat16 or wider, within the bound.
No kernel may reach another device: no remote copies, remote signals or barrier semaphores. Data moves between devices by JAX's collectives and lax.ppermute only.
A program may use at most 64 MiB of HBM per device.

v0:
```python
import math

import jax
import jax.numpy as jnp
from jax import lax
from jax.sharding import PartitionSpec as P


def body(weight, row_factors, col_factors, fitness_ranks):
    members = fitness_ranks.shape[0] * lax.axis_size("pop")
    shaped = fitness_ranks.astype(jnp.float32) / (members - 1) - 0.5
    scaled = (shaped[:, None] * col_factors.astype(jnp.float32)).astype(jnp.bfloat16)
    row_block = lax.all_to_all(row_factors, "pop", split_axis=0, concat_axis=1, tiled=True)
    update = jnp.dot(
        row_block,
        lax.all_gather(scaled, "pop", axis=0, tiled=True),
        preferred_element_type=jnp.float32,
    )
    return weight + 3.0 / math.sqrt(members) * update


def solution(mesh):
    in_specs = (P("pop", "col"), P(None, "pop"), P("pop", "col"), P("pop"))
    out_specs = P("pop", "col")
    return jax.shard_map(body, mesh=mesh, in_specs=in_specs, out_specs=out_specs, check_vma=False)
```

profile of v0, /device:TPU:6, one launch (start us, length us, event | category | flops | bytes accessed | tf_op | source)
XLA Modules:
  0.0 358.1 jit_solution(8198781818060697257)
XLA Ops:
  6.5 0.0 all-gather.2.cloned.1.call-start
  6.5 0.7 multiply_add_fusion
  7.2 1.7 multiply_convert_fusion
  8.9 0.0 all-gather.2.cloned.1.call-update
  8.9 1.3 copy.5
  10.2 52.5 %all_to_all.19 = bf16[48,48,96]{2,1,0:T(8,128)(2,1)S(1)} all-to-all(bf16[48,48,96]{2,1,0:T(8,128)(2,1)S(1)} %bitcast.9), channel_id=1, replica_groups=mesh['pop'=48,'col'=16] {'pop'}, dimensions={0} | all-to-all | bytes 884736 | tf_op jit(solution)/shard_map/all_to_all | solution.py:13
  62.7 0.2 copy.6
  62.9 0.6 all_to_all.17
  63.5 281.7 %all-gather.2.cloned.1.call-done = bf16[4608,1024]{1,0:T(8,128)(2,1)} async-done(((bf16[96,1024]{1,0:T(8,128)(2,1)}), bf16[4608,1024]{1,0:T(8,128)(2,1)}) %all-gather.2.cloned.1.call-update) | async-done | bytes 9437200 | tf_op jit(solution)/shard_map/all_gather | solution.py:16
  345.2 6.1 %fusion.1 = f32[48,1024]{1,0:T(8,128)} fusion(f32[48,1024]{1,0:T(8,128)} %param.4, bf16[48,4608]{1,0:T(8,128)(2,1)S(1)} %all_to_all.17, bf16[4608,1024]{1,0:T(8,128)(2,1)} %all-gather.2.cloned.1.call-done), kind=kOutput, calls=%fused_computation.2 | convolution fusion | flops 453083136 | bytes 10272768 | tf_op jit(solution)/shard_map/dot_general | solution.py:14
Async XLA Ops:
  6.5 338.6 %all-gather.2.cloned.1.call-start = ((), (), s32[]{:S(2)}) async-start(), calls=%async_computation.1 | async-start | bytes 9633792 | tf_op jit(solution)/shard_map/all_gather | solution.py:16
Sparse Core Ops, SparseCore 0:
  9.7 335.3 all-gather.1
where the time goes:
time: 360 us; the launch traced here: 358 us
  waiting for transfers between devices  282 us (78%)
  blocking collectives  52.5 us (15%)
  between operations  13.4 us (4%)
  matrix products  6.11 us (2%)
    all_gather x1, waiting for transfers between devices, body(): lax.all_gather(scaled, 'pop', axis=0, tiled=True)  282 us
    all_to_all x1, blocking collectives, body(): lax.all_to_all(row_factors, 'pop', split_axis=0, concat_axis=1, tiled=True)  52.5 us
  transfers between devices with their start and end apart: 1, of which 1 were waited for; matrix products, arithmetic and copies ran while one was open for 0% of the time, Pallas kernels for 0%

commit v1 on v0

v1 whole, which is shorter than its diff:
```python
import math

import jax
import jax.numpy as jnp
from jax import lax
from jax.sharding import Mesh, PartitionSpec as P

YB, ZB = 2, 3


def body(weight, row_factors, col_factors, fitness_ranks):
    ya, yb, za, zb = (lax.axis_size(a) for a in ("ya", "yb", "za", "zb"))
    members = fitness_ranks.shape[0] * ya * yb * za * zb
    rows, cols = weight.shape
    own = fitness_ranks.shape[0]
    near, far = ("yb", "zb"), ("ya", "za")
    shaped = fitness_ranks.astype(jnp.float32) / (members - 1) - 0.5
    scaled = (shaped[:, None] * col_factors.astype(jnp.float32)).astype(jnp.bfloat16)
    part = row_factors.reshape(ya, yb, za, zb, rows, own).transpose(1, 3, 5, 0, 2, 4)
    part = part.reshape(yb * zb, own, ya * za * rows)
    both = jnp.concatenate([jnp.broadcast_to(scaled, (yb * zb, own, cols)), part], axis=2)
    both = lax.all_to_all(both, near, split_axis=0, concat_axis=0, tiled=True)
    both = both.reshape(yb * zb * own, -1)
    partial = lax.dot_general(
        both[:, cols:], both[:, :cols], (((0,), (0,)), ((), ())), preferred_element_type=jnp.float32
    ).astype(jnp.bfloat16)
    partial = partial.reshape(ya * za, rows, cols)
    partial = lax.all_to_all(partial, far, split_axis=0, concat_axis=0, tiled=True)
    update = jnp.sum(partial.astype(jnp.float32), axis=0)
    return weight + 3.0 / math.sqrt(members) * update


def solution(mesh):
    pop, col = mesh.devices.shape
    fine = Mesh(
        mesh.devices.reshape(8 // YB, YB, 6 // ZB, ZB, col), ("ya", "yb", "za", "zb", "col")
    )
    pop = ("ya", "yb", "za", "zb")
    in_specs = (P(pop, "col"), P(None, pop), P(pop, "col"), P(pop))
    out_specs = P(pop, "col")
    return jax.shard_map(body, mesh=fine, in_specs=in_specs, out_specs=out_specs, check_vma=False)
```

time: 360 us -> 85.1 us (0.24)
  waiting for transfers between devices: 282 us -> 0 us
  blocking collectives: 52.5 us -> 80.5 us
  between operations: 13.4 us -> 0.07 us
  matrix products: 6.11 us -> 0.79 us
    all_gather x1 -> x0, waiting for transfers between devices: 282 us -> none  [body(): lax.all_gather(scaled, 'pop', axis=0, tiled=True)]
    all_to_all x1 -> x2, blocking collectives: 52.5 us -> 80.5 us  [the longest x1 46.7 us: body(): lax.all_to_all(partial, far, split_axis=0, concat_axis=0, tiled=True)]
    dot_general x1, matrix products: 6.11 us -> 0.79 us  [body(): lax.dot_general(both[:, cols:], both[:, :cols], (((0,), (0,)), ((), ())),...]
  transfers between devices with their start and end apart: 1 -> 0, of which waited for: 1 -> 0; matrix products, arithmetic and copies ran while one was open for 0% -> 0% of each run, Pallas kernels for 0% -> 0%
where the time goes in v1:
time: 85.1 us; the launch traced here: 84.9 us
  blocking collectives  80.5 us (95%)
  local copies, waits for them, and re-layouts  1.84 us (2%)
  other arithmetic  1.71 us (2%)
    all_to_all x1, blocking collectives, body(): lax.all_to_all(partial, far, split_axis=0, concat_axis=0, tiled=True)  46.7 us
    all_to_all x1, blocking collectives, body(): both = lax.all_to_all(both, near, split_axis=0, concat_axis=0, tiled=True)  33.7 us

profile of v1, /device:TPU:6, one launch (start us, length us, event | category | flops | bytes accessed | tf_op | source)
XLA Modules:
  0.0 84.9 jit_solution(10418087812965757039)
XLA Ops:
  0.0 0.7 multiply_add_fusion.1
  0.7 0.0 copy-start
  0.7 1.4 %copy.5 = bf16[2304,96]{1,0:T(8,128)(2,1)S(1)} copy(bf16[2304,96]{0,1:T(8,128)(2,1)} %param.5) | data formatting | bytes 884736 | tf_op args[1]
  2.0 0.1 copy.6
  2.1 0.3 copy.7
  2.4 0.0 copy-done
  2.4 0.1 multiply_convert_fusion
  2.5 0.1 broadcast_in_dim.4
  2.6 0.1 pad_maximum_fusion
  2.8 33.7 %all_to_all.10 = bf16[6,96,1408]{2,1,0:T(8,128)(2,1)S(1)} all-to-all(bf16[6,96,1408]{2,1,0:T(8,128)(2,1)S(1)} %pad_maximum_fusion), channel_id=1, replica_groups=mesh['ya'=4,'yb'=2,'za'=2,'zb'=3,'col'=16] {'yb','zb'}, dimensions={0} | all-to-all | bytes 3244032 | tf_op jit(solution)/shard_map/all_to_all | solution.py:22
  36.5 0.8 convolution_convert_fusion
  37.3 0.0 copy-start.1
  37.3 46.7 %all_to_all.11 = bf16[8,48,1024]{2,1,0:T(8,128)(2,1)S(1)} all-to-all(bf16[8,48,1024]{2,1,0:T(8,128)(2,1)S(1)} %bitcast.9), channel_id=1, replica_groups=mesh['ya'=4,'yb'=2,'za'=2,'zb'=3,'col'=16] {'ya','za'}, dimensions={0} | all-to-all | bytes 1572864 | tf_op jit(solution)/shard_map/all_to_all | solution.py:28
  84.0 0.1 convert_reduce_fusion
  84.2 0.0 copy-done.1
  84.2 0.7 multiply_add_fusion
Async XLA Ops:
  0.7 1.7 %copy-start = (bf16[96,1024]{1,0:T(8,128)(2,1)S(1)}, bf16[96,1024]{1,0:T(8,128)(2,1)}, u32[]{:S(2)}) copy-start(bf16[96,1024]{1,0:T(8,128)(2,1)} %param.6) | copy-start | bytes 589828
  37.3 46.9 %copy-start.1 = (f32[48,1024]{1,0:T(8,128)S(1)}, f32[48,1024]{1,0:T(8,128)}, u32[]{:S(2)}) copy-start(f32[48,1024]{1,0:T(8,128)} %param.4) | copy-start | bytes 589828

commit v2 on v1

v2 whole, which is shorter than its diff:
```python
import math

import jax
import jax.numpy as jnp
from jax import lax
from jax.sharding import Mesh, PartitionSpec as P

YB, ZB = 2, 3
NEAR = ("y0", "zb")
ALONG = ("y0", "y2", "y1")


def body(weight, row_factors, col_factors, fitness_ranks):
    size = {a: lax.axis_size(a) for a in ("y2", "y1", "y0", "za", "zb")}
    yb, za, zb = size["y0"], size["za"], size["zb"]
    ys = size["y2"] * size["y1"] * yb
    members = fitness_ranks.shape[0] * ys * za * zb
    rows, cols = weight.shape
    own = fitness_ranks.shape[0]
    half = cols // yb
    shaped = fitness_ranks.astype(jnp.float32) / (members - 1) - 0.5
    scaled = (shaped[:, None] * col_factors.astype(jnp.float32)).astype(jnp.bfloat16)
    scaled = scaled.reshape(own, yb, half).transpose(1, 0, 2)
    scaled = jnp.broadcast_to(scaled, (zb, yb, own, half))
    side = lax.axis_index("za") ^ lax.axis_index("core")
    part = row_factors.reshape(size["y2"], size["y1"], yb, za, zb, rows, own)
    part = lax.dynamic_index_in_dim(part, side, 3, False)
    names = ("y2", "y1", "y0", "zb")
    part = part.transpose(3, 5, *[names.index(a) for a in ALONG], 4).reshape(zb, 1, own, ys * rows)
    part = jnp.broadcast_to(part, (zb, yb, own, ys * rows))
    both = jnp.concatenate([scaled, part], axis=3)
    if NEAR[0] == "y0":
        both = both.transpose(1, 0, 2, 3)
    both = both.reshape(zb * yb, own, -1)
    both = lax.all_to_all(both, NEAR, split_axis=0, concat_axis=0, tiled=True)
    both = both.reshape(zb * yb * own, -1)
    factors = both[:, :half]
    part = lax.all_gather(both[:, half:], "core")

    def product(side):
        out = lax.dot_general(
            part[side], factors, (((0,), (0,)), ((), ())), preferred_element_type=jnp.float32
        )
        return out.astype(jnp.bfloat16).reshape(ys, rows, half)

    def reduce_y(block):
        block = lax.all_to_all(block, ALONG, split_axis=0, concat_axis=0, tiled=True)
        block = block.astype(jnp.float32).reshape([size[a] for a in ALONG] + [rows, half])
        where = ALONG.index("y0")
        return jnp.sum(block, axis=tuple(i for i in range(3) if i != where))

    far, near = product(1), product(0)
    far = reduce_y(far).astype(jnp.bfloat16)
    far, near = lax.optimization_barrier((far, near))
    far = lax.ppermute(far, "za", [(0, 1), (1, 0)])
    update = reduce_y(near) + far.astype(jnp.float32)
    update = update.transpose(1, 0, 2).reshape(rows, cols)
    return weight + 3.0 / math.sqrt(members) * update


def solution(mesh):
    pop, col = mesh.devices.shape
    fine = Mesh(
        mesh.devices.reshape(2, 2, YB, 6 // ZB, ZB, col // 2, 2),
        ("y2", "y1", "y0", "za", "zb", "plane", "core"),
    )
    pop, col = ("y2", "y1", "y0", "za", "zb"), ("plane", "core")
    in_specs = (P(pop, col), P(None, pop), P(pop, col), P(pop))
    out_specs = P(pop, col)
    return jax.shard_map(body, mesh=fine, in_specs=in_specs, out_specs=out_specs, check_vma=False)
```

time: 85.1 us -> 73.3 us (0.86); the launches traced: 84.9 us -> 71.9 us
  blocking collectives: 80.5 us -> 27.6 us
  starting transfers between devices: 0 us -> 21.1 us
  waiting for transfers between devices: 0 us -> 17.2 us
  matrix products: 0.79 us -> 2.48 us
  local copies, waits for them, and re-layouts: 1.84 us -> 0.73 us
  other arithmetic: 1.71 us -> 2.66 us
    all_to_all x2 -> x1, blocking collectives: 80.5 us -> 25.2 us  [body(): both = lax.all_to_all(both, NEAR, split_axis=0, concat_axis=0, tiled=True)]
    all_to_all x0 -> x2, waiting for transfers between devices: none -> 12.3 us  [reduce_y(): lax.all_to_all(block, ALONG, split_axis=0, concat_axis=0, tiled=True)]
    all_to_all x0 -> x2, starting transfers between devices: none -> 10.9 us  [reduce_y(): lax.all_to_all(block, ALONG, split_axis=0, concat_axis=0, tiled=True)]
    ppermute x0 -> x1, starting transfers between devices: none -> 10.3 us  [body(): far = lax.ppermute(far, 'za', [(0, 1), (1, 0)])]
    ppermute x0 -> x1, waiting for transfers between devices: none -> 4.87 us  [body(): far = lax.ppermute(far, 'za', [(0, 1), (1, 0)])]
    all_gather x0 -> x1, blocking collectives: none -> 2.44 us  [body(): part = lax.all_gather(both[:, half:], 'core')]
    dot_general x1 -> x2, matrix products: 0.79 us -> 2.48 us  [product(): lax.dot_general(part[side], factors, (((0,), (0,)), ((), ())), preferred_...]
    unnamed x5, local copies, waits for them, and re-layouts: 1.37 us -> 0.32 us
  transfers between devices with their start and end apart: 0 -> 3, of which waited for: 0 -> 3; matrix products, arithmetic and copies ran while one was open for 0% -> 2% of each run, Pallas kernels for 0% -> 0%
where the time goes in v2:
time: 73.3 us; the launch traced here: 71.9 us
  blocking collectives  27.6 us (38%)
  starting transfers between devices  21.1 us (29%)
  waiting for transfers between devices  17.2 us (23%)
  other arithmetic  2.66 us (4%)
  matrix products  2.48 us (3%)
    all_to_all x1, blocking collectives, body(): both = lax.all_to_all(both, NEAR, split_axis=0, concat_axis=0, tiled=True)  25.2 us
    all_to_all x2, waiting for transfers between devices, reduce_y(): lax.all_to_all(block, ALONG, split_axis=0, concat_axis=0, tiled=True)  12.3 us
    all_to_all x2, starting transfers between devices, reduce_y(): lax.all_to_all(block, ALONG, split_axis=0, concat_axis=0, tiled=True)  10.9 us
    ppermute x1, starting transfers between devices, body(): far = lax.ppermute(far, 'za', [(0, 1), (1, 0)])  10.3 us
    ppermute x1, waiting for transfers between devices, body(): far = lax.ppermute(far, 'za', [(0, 1), (1, 0)])  4.87 us
    dot_general x2, matrix products, product(): lax.dot_general(part[side], factors, (((0,), (0,)), ((), ())), preferred_...  2.48 us
    all_gather x1, blocking collectives, body(): part = lax.all_gather(both[:, half:], 'core')  2.44 us
  transfers between devices with their start and end apart: 3, of which 3 were waited for; matrix products, arithmetic and copies ran while one was open for 2% of the time, Pallas kernels for 0%

profile of v2, /device:TPU:6, one launch (start us, length us, event | category | flops | bytes accessed | tf_op | source)
XLA Modules:
  0.0 71.9 jit_solution(10414425984505824855)
XLA Ops:
  0.0 0.0 copy-start
  0.0 0.7 multiply_add_fusion
  0.7 1.0 %multiply_convert_fusion = bf16[96,1024]{1,0:T(8,128)(2,1)S(1)} fusion(bf16[96,1024]{1,0:T(8,128)(2,1)} %param.6, f32[96]{0:T(128)S(1)} %multiply_add_fusion), kind=kLoop, calls=%fused_computation.9 | loop fusion | flops 294912 | bytes 393600 | tf_op jit(solution)/shard_map/convert_element_type | solution.py:22
  1.8 0.0 copy-done
  1.8 0.3 copy.18
  2.2 0.2 copy.20
  2.5 0.1 pad_maximum_fusion
  2.6 25.2 %all_to_all.15 = bf16[6,96,896]{2,1,0:T(8,128)(2,1)S(1)} all-to-all(bf16[6,96,896]{2,1,0:T(8,128)(2,1)S(1)} %bitcast.28), channel_id=1, replica_groups=mesh['y2'=2,'y1'=2,'y0'=2,'za'=2,'zb'=3,'plane'=8,'core'=2] {'y0','zb'}, dimensions={0} | all-to-all | bytes 2064384 | tf_op jit(solution)/shard_map/all_to_all | solution.py:35
  27.8 2.4 %all-gather = bf16[1152,384]{1,0:T(8,128)(2,1)S(1)} all-gather(bf16[576,384]{1,0:T(8,128)(2,1)S(1)} %slice.18), channel_id=2, replica_groups=mesh['y2'=2,'y1'=2,'y0'=2,'za'=2,'zb'=3,'plane'=8,'core'=2] {'core'}, dimensions={0}, use_global_device_ids=true | all-gather | bytes 1327104 | tf_op jit(solution)/shard_map/all_gather | solution.py:38
  30.2 1.2 %convolution_convert_fusion.1 = bf16[384,512]{1,0:T(8,128)(2,1)} fusion(bf16[576,896]{1,0:T(8,128)(2,1)S(1)} %bitcast.30, bf16[1152,384]{1,0:T(8,128)(2,1)S(1)} %all-gather), kind=kOutput, calls=%fused_computation.1 | convolution fusion | flops 226689024 | bytes 1425408 | tf_op jit(solution)/shard_map/dot_general | solution.py:41
  31.4 6.2 %all-to-all-start.1 = ((bf16[8,48,512]{2,1,0:T(8,128)(2,1)}), bf16[8,48,512]{2,1,0:T(8,128)(2,1)S(1)}, u32[]{:S(2)}, u32[]{:S(2)}) async-start(bf16[8,48,512]{2,1,0:T(8,128)(2,1)} %bitcast.8), calls=%async_computation.1 | async-start | bytes 786432 | tf_op jit(solution)/shard_map/all_to_all | solution.py:47
  37.6 1.2 %convolution_convert_fusion = bf16[384,512]{1,0:T(8,128)(2,1)} fusion(bf16[576,896]{1,0:T(8,128)(2,1)S(1)} %bitcast.31, bf16[1152,384]{1,0:T(8,128)(2,1)S(1)} %all-gather), kind=kOutput, calls=%fused_computation | convolution fusion | flops 226689024 | bytes 1425408 | tf_op jit(solution)/shard_map/dot_general | solution.py:41
  38.9 11.1 %all-to-all-done.1 = bf16[8,48,512]{2,1,0:T(8,128)(2,1)S(1)} async-done(((bf16[8,48,512]{2,1,0:T(8,128)(2,1)}), bf16[8,48,512]{2,1,0:T(8,128)(2,1)S(1)}, u32[]{:S(2)}, u32[]{:S(2)}) %all-to-all-start.1) | async-done | bytes 393248 | tf_op jit(solution)/shard_map/all_to_all | solution.py:47
  50.0 0.1 bitcast_reduce_fusion
  50.0 0.0 copy-start.1
  50.0 4.7 %all-to-all-start.2 = ((bf16[8,48,512]{2,1,0:T(8,128)(2,1)}), bf16[8,48,512]{2,1,0:T(8,128)(2,1)S(1)}, u32[]{:S(2)}, u32[]{:S(2)}) async-start(bf16[8,48,512]{2,1,0:T(8,128)(2,1)} %bitcast.10), calls=%async_computation.2 | async-start | bytes 786432 | tf_op jit(solution)/shard_map/all_to_all | solution.py:47
  54.7 10.3 %collective-permute-start = (bf16[2,48,512]{2,1,0:T(8,128)(2,1)S(1)}, bf16[2,48,512]{2,1,0:T(8,128)(2,1)S(1)}, u32[]{:S(2)}, u32[]{:S(2)}) collective-permute-start(bf16[2,48,512]{2,1,0:T(8,128)(2,1)S(1)} %bitcast_reduce_fusion), channel_id=1, source_target_pairs={{0,48},{48,0},{1,49},{49,1},{2,50},{50,2},{3,51},{51,3},{4,52},{52... | collective-permute-start | bytes 294920 | tf_op jit(solution)/shard_map/ppermute | solution.py:55
  65.0 1.2 %all-to-all-done.2 = bf16[8,48,512]{2,1,0:T(8,128)(2,1)S(1)} async-done(((bf16[8,48,512]{2,1,0:T(8,128)(2,1)}), bf16[8,48,512]{2,1,0:T(8,128)(2,1)S(1)}, u32[]{:S(2)}, u32[]{:S(2)}) %all-to-all-start.2) | async-done | bytes 393248 | tf_op jit(solution)/shard_map/all_to_all | solution.py:47
  66.2 0.1 convert_reduce_fusion
  66.3 4.9 %collective-permute-done = bf16[2,48,512]{2,1,0:T(8,128)(2,1)S(1)} collective-permute-done((bf16[2,48,512]{2,1,0:T(8,128)(2,1)S(1)}, bf16[2,48,512]{2,1,0:T(8,128)(2,1)S(1)}, u32[]{:S(2)}, u32[]{:S(2)}) %collective-permute-start) | collective-permute-done | bytes 98336 | tf_op jit(solution)/shard_map/ppermute | solution.py:55
  71.2 0.0 copy-done.1
  71.2 0.7 add.13
  (8 shorter events, 0.2 us)
Async XLA Ops:
  0.0 1.8 %copy-start = (bf16[2304,96]{0,1:T(8,128)(2,1)S(1)}, bf16[2304,96]{0,1:T(8,128)(2,1)}, u32[]{:S(2)}) copy-start(bf16[2304,96]{0,1:T(8,128)(2,1)} %param.5) | copy-start | bytes 1327108
  31.4 18.5 %all-to-all-start.1 = ((bf16[8,48,512]{2,1,0:T(8,128)(2,1)}), bf16[8,48,512]{2,1,0:T(8,128)(2,1)S(1)}, u32[]{:S(2)}, u32[]{:S(2)}) async-start(bf16[8,48,512]{2,1,0:T(8,128)(2,1)} %bitcast.8), calls=%async_computation.1 | async-start | bytes 786432 | tf_op jit(solution)/shard_map/all_to_all | solution.py:47
  50.0 21.2 %copy-start.1 = (f32[48,1024]{1,0:T(8,128)S(1)}, f32[48,1024]{1,0:T(8,128)}, u32[]{:S(2)}) copy-start(f32[48,1024]{1,0:T(8,128)} %param.4) | copy-start | bytes 589828
  50.0 16.2 %all-to-all-start.2 = ((bf16[8,48,512]{2,1,0:T(8,128)(2,1)}), bf16[8,48,512]{2,1,0:T(8,128)(2,1)S(1)}, u32[]{:S(2)}, u32[]{:S(2)}) async-start(bf16[8,48,512]{2,1,0:T(8,128)(2,1)} %bitcast.10), calls=%async_computation.2 | async-start | bytes 786432 | tf_op jit(solution)/shard_map/all_to_all | solution.py:47
  54.7 16.4 %collective-permute-start = (bf16[2,48,512]{2,1,0:T(8,128)(2,1)S(1)}, bf16[2,48,512]{2,1,0:T(8,128)(2,1)S(1)}, u32[]{:S(2)}, u32[]{:S(2)}) collective-permute-start(bf16[2,48,512]{2,1,0:T(8,128)(2,1)S(1)} %bitcast_reduce_fusion), channel_id=1, source_target_pairs={{0,48},{48,0},{1,49},{49,1},{2,50},{50,2},{3,51},{51,3},{4,52},{52... | collective-permute-start | bytes 294920 | tf_op jit(solution)/shard_map/ppermute | solution.py:55

commit v3 on v2

--- a/solution.py
+++ b/solution.py
@@ -7,7 +7,8 @@
 
 YB, ZB = 2, 3
 NEAR = ("y0", "zb")
-ALONG = ("y0", "y2", "y1")
+PARTNER = (1, 0, 2)
+ALONG = ("y1", "y2", "y0")
 
 
 def body(weight, row_factors, col_factors, fitness_ranks):
@@ -22,9 +23,12 @@
     scaled = (shaped[:, None] * col_factors.astype(jnp.float32)).astype(jnp.bfloat16)
     scaled = scaled.reshape(own, yb, half).transpose(1, 0, 2)
     scaled = jnp.broadcast_to(scaled, (zb, yb, own, half))
-    side = lax.axis_index("za") ^ lax.axis_index("core")
+    here = lax.axis_index("za")
     part = row_factors.reshape(size["y2"], size["y1"], yb, za, zb, rows, own)
-    part = lax.dynamic_index_in_dim(part, side, 3, False)
+    there = lax.dynamic_index_in_dim(part, 1 - here, 3, False)
+    there = jnp.stack([there[:, :, :, z] for z in PARTNER], axis=3)
+    part = lax.dynamic_index_in_dim(part, here, 3, False)
+    part = jnp.where(lax.axis_index("core") == 0, part, there)
     names = ("y2", "y1", "y0", "zb")
     part = part.transpose(3, 5, *[names.index(a) for a in ALONG], 4).reshape(zb, 1, own, ys * rows)
     part = jnp.broadcast_to(part, (zb, yb, own, ys * rows))
@@ -49,10 +53,11 @@
         where = ALONG.index("y0")
         return jnp.sum(block, axis=tuple(i for i in range(3) if i != where))
 
+    pairs = [(z, zb + PARTNER[z]) for z in range(zb)] + [(zb + PARTNER[z], z) for z in range(zb)]
     far, near = product(1), product(0)
     far = reduce_y(far).astype(jnp.bfloat16)
     far, near = lax.optimization_barrier((far, near))
-    far = lax.ppermute(far, "za", [(0, 1), (1, 0)])
+    far = lax.ppermute(far, ("za", "zb"), pairs)
     update = reduce_y(near) + far.astype(jnp.float32)
     update = update.transpose(1, 0, 2).reshape(rows, cols)
     return weight + 3.0 / math.sqrt(members) * update

time: 73.3 us -> 70.6 us (0.963)
  waiting for transfers between devices: 17.2 us -> 15.1 us
    ppermute x1, waiting for transfers between devices: 4.87 us -> 2.45 us  [body(): far = lax.ppermute(far, ('za', 'zb'), pairs)]
where the time goes in v3:
time: 70.6 us; the launch traced here: 69.7 us
  blocking collectives  27.6 us (39%)
  starting transfers between devices  20.9 us (30%)
  waiting for transfers between devices  15.1 us (21%)
  other arithmetic  2.75 us (4%)
  matrix products  2.5 us (4%)
  local copies, waits for them, and re-layouts  0.75 us (1%)
    all_to_all x1, blocking collectives, body(): both = lax.all_to_all(both, NEAR, split_axis=0, concat_axis=0, tiled=True)  25.2 us
    all_to_all x2, waiting for transfers between devices, reduce_y(): lax.all_to_all(block, ALONG, split_axis=0, concat_axis=0, tiled=True)  12.6 us
    all_to_all x2, starting transfers between devices, reduce_y(): lax.all_to_all(block, ALONG, split_axis=0, concat_axis=0, tiled=True)  10.5 us
    ppermute x1, starting transfers between devices, body(): far = lax.ppermute(far, ('za', 'zb'), pairs)  10.4 us
    dot_general x2, matrix products, product(): lax.dot_general(part[side], factors, (((0,), (0,)), ((), ())), preferred_...  2.5 us
    ppermute x1, waiting for transfers between devices, body(): far = lax.ppermute(far, ('za', 'zb'), pairs)  2.45 us
    all_gather x1, blocking collectives, body(): part = lax.all_gather(both[:, half:], 'core')  2.44 us
  transfers between devices with their start and end apart: 3, of which 3 were waited for; matrix products, arithmetic and copies ran while one was open for 2% of the time, Pallas kernels for 0%

profile of v3, /device:TPU:6, one launch (start us, length us, event | category | flops | bytes accessed | tf_op | source)
XLA Modules:
  0.0 69.7 jit_solution(8707965937526251177)
XLA Ops:
  0.0 0.0 copy-start
  0.0 0.7 %multiply_add_fusion = f32[96]{0:T(128)S(1)} fusion(s32[96]{0:T(128)} %param.7), kind=kLoop, calls=%fused_computation.14 | loop fusion | flops 288 | bytes 768 | tf_op jit(solution)/shard_map/sub | solution.py:22
  0.7 1.0 %multiply_convert_fusion = bf16[96,1024]{1,0:T(8,128)(2,1)S(1)} fusion(bf16[96,1024]{1,0:T(8,128)(2,1)} %param.6, f32[96]{0:T(128)S(1)} %multiply_add_fusion), kind=kLoop, calls=%fused_computation.8 | loop fusion | flops 294912 | bytes 393600 | tf_op jit(solution)/shard_map/convert_element_type | solution.py:23
  1.8 0.0 copy-done
  1.8 0.3 copy.18
  2.2 0.1 fusion.4
  2.3 0.2 copy.20
  2.6 0.1 pad_maximum_fusion
  2.7 25.2 %all_to_all.15 = bf16[6,96,896]{2,1,0:T(8,128)(2,1)S(1)} all-to-all(bf16[6,96,896]{2,1,0:T(8,128)(2,1)S(1)} %bitcast.28), channel_id=1, replica_groups=mesh['y2'=2,'y1'=2,'y0'=2,'za'=2,'zb'=3,'plane'=8,'core'=2] {'y0','zb'}, dimensions={0} | all-to-all | bytes 2064384 | tf_op jit(solution)/shard_map/all_to_all | solution.py:39
  27.9 2.4 %all-gather = bf16[1152,384]{1,0:T(8,128)(2,1)S(1)} all-gather(bf16[576,384]{1,0:T(8,128)(2,1)S(1)} %slice.33), channel_id=2, replica_groups=mesh['y2'=2,'y1'=2,'y0'=2,'za'=2,'zb'=3,'plane'=8,'core'=2] {'core'}, dimensions={0}, use_global_device_ids=true | all-gather | bytes 1327104 | tf_op jit(solution)/shard_map/all_gather | solution.py:42
  30.3 1.2 %convolution_convert_fusion.1 = bf16[384,512]{1,0:T(8,128)(2,1)} fusion(bf16[576,896]{1,0:T(8,128)(2,1)S(1)} %bitcast.32, bf16[1152,384]{1,0:T(8,128)(2,1)S(1)} %all-gather), kind=kOutput, calls=%fused_computation.1 | convolution fusion | flops 226689024 | bytes 1425408 | tf_op jit(solution)/shard_map/dot_general | solution.py:45
  31.6 6.2 %all-to-all-start.1 = ((bf16[8,48,512]{2,1,0:T(8,128)(2,1)}), bf16[8,48,512]{2,1,0:T(8,128)(2,1)S(1)}, u32[]{:S(2)}, u32[]{:S(2)}) async-start(bf16[8,48,512]{2,1,0:T(8,128)(2,1)} %bitcast.9), calls=%async_computation.1 | async-start | bytes 786432 | tf_op jit(solution)/shard_map/all_to_all | solution.py:51
  37.8 1.3 %convolution_convert_fusion = bf16[384,512]{1,0:T(8,128)(2,1)} fusion(bf16[576,896]{1,0:T(8,128)(2,1)S(1)} %bitcast.33, bf16[1152,384]{1,0:T(8,128)(2,1)S(1)} %all-gather), kind=kOutput, calls=%fused_computation | convolution fusion | flops 226689024 | bytes 1425408 | tf_op jit(solution)/shard_map/dot_general | solution.py:45
  39.0 11.5 %all-to-all-done.1 = bf16[8,48,512]{2,1,0:T(8,128)(2,1)S(1)} async-done(((bf16[8,48,512]{2,1,0:T(8,128)(2,1)}), bf16[8,48,512]{2,1,0:T(8,128)(2,1)S(1)}, u32[]{:S(2)}, u32[]{:S(2)}) %all-to-all-start.1) | async-done | bytes 393248 | tf_op jit(solution)/shard_map/all_to_all | solution.py:51
  50.5 0.1 reduce
  50.6 0.0 copy-start.1
  50.6 4.3 %all-to-all-start.2 = ((bf16[8,48,512]{2,1,0:T(8,128)(2,1)}), bf16[8,48,512]{2,1,0:T(8,128)(2,1)S(1)}, u32[]{:S(2)}, u32[]{:S(2)}) async-start(bf16[8,48,512]{2,1,0:T(8,128)(2,1)} %bitcast.11), calls=%async_computation.2 | async-start | bytes 786432 | tf_op jit(solution)/shard_map/all_to_all | solution.py:51
  54.8 10.4 %collective-permute-start = (bf16[2,48,512]{2,1,0:T(8,128)(2,1)S(1)}, bf16[2,48,512]{2,1,0:T(8,128)(2,1)S(1)}, u32[]{:S(2)}, u32[]{:S(2)}) collective-permute-start(bf16[2,48,512]{2,1,0:T(8,128)(2,1)S(1)} %reduce), channel_id=1, source_target_pairs={{0,64},{16,48},{32,80},{64,0},{48,16},{80,32},{1,65},{17,49},{33,8... | collective-permute-start | bytes 294920 | tf_op jit(solution)/shard_map/ppermute | solution.py:60
  65.3 1.1 %all-to-all-done.2 = bf16[8,48,512]{2,1,0:T(8,128)(2,1)S(1)} async-done(((bf16[8,48,512]{2,1,0:T(8,128)(2,1)}), bf16[8,48,512]{2,1,0:T(8,128)(2,1)S(1)}, u32[]{:S(2)}, u32[]{:S(2)}) %all-to-all-start.2) | async-done | bytes 393248 | tf_op jit(solution)/shard_map/all_to_all | solution.py:51
  66.4 0.1 convert_reduce_fusion
  66.5 2.4 %collective-permute-done = bf16[2,48,512]{2,1,0:T(8,128)(2,1)S(1)} collective-permute-done((bf16[2,48,512]{2,1,0:T(8,128)(2,1)S(1)}, bf16[2,48,512]{2,1,0:T(8,128)(2,1)S(1)}, u32[]{:S(2)}, u32[]{:S(2)}) %collective-permute-start) | collective-permute-done | bytes 98336 | tf_op jit(solution)/shard_map/ppermute | solution.py:60
  69.0 0.0 copy-done.1
  69.0 0.7 %add.18 = f32[48,1024]{1,0:T(8,128)} add(f32[48,1024]{1,0:T(8,128)S(1)} %copy-done.1, f32[48,1024]{1,0:T(8,128)S(1)} %bitcast.39) | non-fusion elementwise | flops 49152 | bytes 589824 | tf_op jit(solution)/shard_map/add | solution.py:63
  (9 shorter events, 0.3 us)
Async XLA Ops:
  0.0 1.8 %copy-start = (bf16[2304,96]{0,1:T(8,128)(2,1)S(1)}, bf16[2304,96]{0,1:T(8,128)(2,1)}, u32[]{:S(2)}) copy-start(bf16[2304,96]{0,1:T(8,128)(2,1)} %param.5) | copy-start | bytes 1327108
  31.6 18.9 %all-to-all-start.1 = ((bf16[8,48,512]{2,1,0:T(8,128)(2,1)}), bf16[8,48,512]{2,1,0:T(8,128)(2,1)S(1)}, u32[]{:S(2)}, u32[]{:S(2)}) async-start(bf16[8,48,512]{2,1,0:T(8,128)(2,1)} %bitcast.9), calls=%async_computation.1 | async-start | bytes 786432 | tf_op jit(solution)/shard_map/all_to_all | solution.py:51
  50.6 18.4 %copy-start.1 = (f32[48,1024]{1,0:T(8,128)S(1)}, f32[48,1024]{1,0:T(8,128)}, u32[]{:S(2)}) copy-start(f32[48,1024]{1,0:T(8,128)} %param.4) | copy-start | bytes 589828
  50.6 15.9 %all-to-all-start.2 = ((bf16[8,48,512]{2,1,0:T(8,128)(2,1)}), bf16[8,48,512]{2,1,0:T(8,128)(2,1)S(1)}, u32[]{:S(2)}, u32[]{:S(2)}) async-start(bf16[8,48,512]{2,1,0:T(8,128)(2,1)} %bitcast.11), calls=%async_computation.2 | async-start | bytes 786432 | tf_op jit(solution)/shard_map/all_to_all | solution.py:51
  54.8 14.1 %collective-permute-start = (bf16[2,48,512]{2,1,0:T(8,128)(2,1)S(1)}, bf16[2,48,512]{2,1,0:T(8,128)(2,1)S(1)}, u32[]{:S(2)}, u32[]{:S(2)}) collective-permute-start(bf16[2,48,512]{2,1,0:T(8,128)(2,1)S(1)} %reduce), channel_id=1, source_target_pairs={{0,64},{16,48},{32,80},{64,0},{48,16},{80,32},{1,65},{17,49},{33,8... | collective-permute-start | bytes 294920 | tf_op jit(solution)/shard_map/ppermute | solution.py:60

commit v4 on v3

--- a/solution.py
+++ b/solution.py
@@ -7,6 +7,7 @@
 
 YB, ZB = 2, 3
 NEAR = ("y0", "zb")
+NEAR_ORDER = (1, 2, 0, 4, 5, 3)
 PARTNER = (1, 0, 2)
 ALONG = ("y1", "y2", "y0")
 
@@ -29,6 +30,7 @@
     there = jnp.stack([there[:, :, :, z] for z in PARTNER], axis=3)
     part = lax.dynamic_index_in_dim(part, here, 3, False)
     part = jnp.where(lax.axis_index("core") == 0, part, there)
+    part = jnp.stack([part[:, :, :, z] for z in NEAR_ORDER[:zb]], axis=3)
     names = ("y2", "y1", "y0", "zb")
     part = part.transpose(3, 5, *[names.index(a) for a in ALONG], 4).reshape(zb, 1, own, ys * rows)
     part = jnp.broadcast_to(part, (zb, yb, own, ys * rows))
@@ -36,7 +38,9 @@
     if NEAR[0] == "y0":
         both = both.transpose(1, 0, 2, 3)
     both = both.reshape(zb * yb, own, -1)
-    both = lax.all_to_all(both, NEAR, split_axis=0, concat_axis=0, tiled=True)
+    both = lax.all_to_all(
+        both, NEAR, split_axis=0, concat_axis=0, tiled=True, axis_index_groups=[NEAR_ORDER]
+    )
     both = both.reshape(zb * yb * own, -1)
     factors = both[:, :half]
     part = lax.all_gather(both[:, half:], "core")

time: 70.6 us -> 69.4 us (0.983)
  local copies, waits for them, and re-layouts: 0.75 us -> 2.55 us
  other arithmetic: 2.75 us -> 1.18 us
  blocking collectives: 27.6 us -> 26.6 us
    unnamed x5 -> x7, local copies, waits for them, and re-layouts: 0.32 us -> 2.09 us
    all_to_all x1, blocking collectives: 25.2 us -> 24.2 us  [body(): lax.all_to_all(both, NEAR, split_axis=0, concat_axis=0, tiled=True, axis_...]
    convert_element_type x1, other arithmetic: 1.03 us -> 0.1 us  [body(): (shaped[:, None] * col_factors.astype(jnp.float32)).astype(jnp.bfloat16)]
    sub x1, other arithmetic: 0.71 us -> 0.01 us  [body(): shaped = fitness_ranks.astype(jnp.float32) / (members - 1) - 0.5]
where the time goes in v4:
time: 69.4 us; the launch traced here: 69 us
  blocking collectives  26.6 us (38%)
  starting transfers between devices  20.7 us (30%)
  waiting for transfers between devices  15.3 us (22%)
  local copies, waits for them, and re-layouts  2.55 us (4%)
  matrix products  2.5 us (4%)
  other arithmetic  1.18 us (2%)
    all_to_all x1, blocking collectives, body(): lax.all_to_all(both, NEAR, split_axis=0, concat_axis=0, tiled=True, axis_...  24.2 us
    all_to_all x2, waiting for transfers between devices, reduce_y(): lax.all_to_all(block, ALONG, split_axis=0, concat_axis=0, tiled=True)  12.8 us
    all_to_all x2, starting transfers between devices, reduce_y(): lax.all_to_all(block, ALONG, split_axis=0, concat_axis=0, tiled=True)  10.5 us
    ppermute x1, starting transfers between devices, body(): far = lax.ppermute(far, ('za', 'zb'), pairs)  10.2 us
    dot_general x2, matrix products, product(): lax.dot_general(part[side], factors, (((0,), (0,)), ((), ())), preferred_...  2.5 us
    ppermute x1, waiting for transfers between devices, body(): far = lax.ppermute(far, ('za', 'zb'), pairs)  2.47 us
    all_gather x1, blocking collectives, body(): part = lax.all_gather(both[:, half:], 'core')  2.44 us
    unnamed x7, local copies, waits for them, and re-layouts  2.09 us
  transfers between devices with their start and end apart: 3, of which 3 were waited for; matrix products, arithmetic and copies ran while one was open for 2% of the time, Pallas kernels for 0%

profile of v4, /device:TPU:6, one launch (start us, length us, event | category | flops | bytes accessed | tf_op | source)
XLA Modules:
  0.0 69.0 jit_solution(12890199075337001303)
XLA Ops:
  0.0 1.3 %copy.18 = bf16[2304,96]{1,0:T(8,128)(2,1)S(1)} copy(bf16[2304,96]{0,1:T(8,128)(2,1)} %param.5) | data formatting | bytes 884736 | tf_op args[1]
  1.4 0.0 copy-start.2
  1.4 0.0 copy-start
  1.4 0.1 maximum_select_fusion
  1.5 0.5 copy-done.2
  2.0 0.3 copy-done
  2.3 0.1 multiply_convert_fusion
  2.4 0.1 maximum_bitcast_fusion
  2.5 0.2 copy.20
  2.8 0.1 pad_maximum_fusion
  2.9 24.2 %all_to_all.15 = bf16[6,96,896]{2,1,0:T(8,128)(2,1)S(1)} all-to-all(bf16[6,96,896]{2,1,0:T(8,128)(2,1)S(1)} %bitcast.28), channel_id=1, replica_groups={{16,32,0,112,128,96},{17,33,1,113,129,97},{18,34,2,114,130,98},{19,35,3..., dimensions={0} | all-to-all | bytes 2064384 | tf_op jit(solution)/shard_map/all_to_all | solution.py:41
  27.2 2.4 %all-gather = bf16[1152,384]{1,0:T(8,128)(2,1)S(1)} all-gather(bf16[576,384]{1,0:T(8,128)(2,1)S(1)} %slice.45), channel_id=2, replica_groups=mesh['y2'=2,'y1'=2,'y0'=2,'za'=2,'zb'=3,'plane'=8,'core'=2] {'core'}, dimensions={0}, use_global_device_ids=true | all-gather | bytes 1327104 | tf_op jit(solution)/shard_map/all_gather | solution.py:46
  29.6 1.2 %convolution_convert_fusion.1 = bf16[384,512]{1,0:T(8,128)(2,1)} fusion(bf16[576,896]{1,0:T(8,128)(2,1)S(1)} %bitcast.32, bf16[1152,384]{1,0:T(8,128)(2,1)S(1)} %all-gather), kind=kOutput, calls=%fused_computation.1 | convolution fusion | flops 226689024 | bytes 1425408 | tf_op jit(solution)/shard_map/dot_general | solution.py:49
  30.8 6.2 %all-to-all-start.1 = ((bf16[8,48,512]{2,1,0:T(8,128)(2,1)}), bf16[8,48,512]{2,1,0:T(8,128)(2,1)S(1)}, u32[]{:S(2)}, u32[]{:S(2)}) async-start(bf16[8,48,512]{2,1,0:T(8,128)(2,1)} %bitcast.9), calls=%async_computation.1 | async-start | bytes 786432 | tf_op jit(solution)/shard_map/all_to_all | solution.py:55
  37.0 1.3 %convolution_convert_fusion = bf16[384,512]{1,0:T(8,128)(2,1)} fusion(bf16[576,896]{1,0:T(8,128)(2,1)S(1)} %bitcast.33, bf16[1152,384]{1,0:T(8,128)(2,1)S(1)} %all-gather), kind=kOutput, calls=%fused_computation | convolution fusion | flops 226689024 | bytes 1425408 | tf_op jit(solution)/shard_map/dot_general | solution.py:49
  38.3 11.5 %all-to-all-done.1 = bf16[8,48,512]{2,1,0:T(8,128)(2,1)S(1)} async-done(((bf16[8,48,512]{2,1,0:T(8,128)(2,1)}), bf16[8,48,512]{2,1,0:T(8,128)(2,1)S(1)}, u32[]{:S(2)}, u32[]{:S(2)}) %all-to-all-start.1) | async-done | bytes 393248 | tf_op jit(solution)/shard_map/all_to_all | solution.py:55
  49.8 0.1 reduce
  49.8 0.0 copy-start.1
  49.8 4.3 %all-to-all-start.2 = ((bf16[8,48,512]{2,1,0:T(8,128)(2,1)}), bf16[8,48,512]{2,1,0:T(8,128)(2,1)S(1)}, u32[]{:S(2)}, u32[]{:S(2)}) async-start(bf16[8,48,512]{2,1,0:T(8,128)(2,1)} %bitcast.11), calls=%async_computation.2 | async-start | bytes 786432 | tf_op jit(solution)/shard_map/all_to_all | solution.py:55
  54.1 10.2 %collective-permute-start = (bf16[2,48,512]{2,1,0:T(8,128)(2,1)S(1)}, bf16[2,48,512]{2,1,0:T(8,128)(2,1)S(1)}, u32[]{:S(2)}, u32[]{:S(2)}) collective-permute-start(bf16[2,48,512]{2,1,0:T(8,128)(2,1)S(1)} %reduce), channel_id=1, source_target_pairs={{0,64},{16,48},{32,80},{64,0},{48,16},{80,32},{1,65},{17,49},{33,8... | collective-permute-start | bytes 294920 | tf_op jit(solution)/shard_map/ppermute | solution.py:64
  64.3 1.4 %all-to-all-done.2 = bf16[8,48,512]{2,1,0:T(8,128)(2,1)S(1)} async-done(((bf16[8,48,512]{2,1,0:T(8,128)(2,1)}), bf16[8,48,512]{2,1,0:T(8,128)(2,1)S(1)}, u32[]{:S(2)}, u32[]{:S(2)}) %all-to-all-start.2) | async-done | bytes 393248 | tf_op jit(solution)/shard_map/all_to_all | solution.py:55
  65.7 0.1 convert_reduce_fusion
  65.7 2.5 %collective-permute-done = bf16[2,48,512]{2,1,0:T(8,128)(2,1)S(1)} collective-permute-done((bf16[2,48,512]{2,1,0:T(8,128)(2,1)S(1)}, bf16[2,48,512]{2,1,0:T(8,128)(2,1)S(1)}, u32[]{:S(2)}, u32[]{:S(2)}) %collective-permute-start) | collective-permute-done | bytes 98336 | tf_op jit(solution)/shard_map/ppermute | solution.py:64
  68.3 0.0 copy-done.1
  68.3 0.7 %add.18 = f32[48,1024]{1,0:T(8,128)} add(f32[48,1024]{1,0:T(8,128)S(1)} %copy-done.1, f32[48,1024]{1,0:T(8,128)S(1)} %bitcast.39) | non-fusion elementwise | flops 49152 | bytes 589824 | tf_op jit(solution)/shard_map/add | solution.py:67
  (12 shorter events, 0.3 us)
Async XLA Ops:
  1.4 0.7 copy-start.2
  1.4 0.9 %copy-start = (bf16[96,1024]{1,0:T(8,128)(2,1)S(1)}, bf16[96,1024]{1,0:T(8,128)(2,1)}, u32[]{:S(2)}) copy-start(bf16[96,1024]{1,0:T(8,128)(2,1)} %param.6) | copy-start | bytes 589828
  30.8 18.9 %all-to-all-start.1 = ((bf16[8,48,512]{2,1,0:T(8,128)(2,1)}), bf16[8,48,512]{2,1,0:T(8,128)(2,1)S(1)}, u32[]{:S(2)}, u32[]{:S(2)}) async-start(bf16[8,48,512]{2,1,0:T(8,128)(2,1)} %bitcast.9), calls=%async_computation.1 | async-start | bytes 786432 | tf_op jit(solution)/shard_map/all_to_all | solution.py:55
  49.8 18.4 %copy-start.1 = (f32[48,1024]{1,0:T(8,128)S(1)}, f32[48,1024]{1,0:T(8,128)}, u32[]{:S(2)}) copy-start(f32[48,1024]{1,0:T(8,128)} %param.4) | copy-start | bytes 589828
  49.8 15.8 %all-to-all-start.2 = ((bf16[8,48,512]{2,1,0:T(8,128)(2,1)}), bf16[8,48,512]{2,1,0:T(8,128)(2,1)S(1)}, u32[]{:S(2)}, u32[]{:S(2)}) async-start(bf16[8,48,512]{2,1,0:T(8,128)(2,1)} %bitcast.11), calls=%async_computation.2 | async-start | bytes 786432 | tf_op jit(solution)/shard_map/all_to_all | solution.py:55
  54.1 14.1 %collective-permute-start = (bf16[2,48,512]{2,1,0:T(8,128)(2,1)S(1)}, bf16[2,48,512]{2,1,0:T(8,128)(2,1)S(1)}, u32[]{:S(2)}, u32[]{:S(2)}) collective-permute-start(bf16[2,48,512]{2,1,0:T(8,128)(2,1)S(1)} %reduce), channel_id=1, source_target_pairs={{0,64},{16,48},{32,80},{64,0},{48,16},{80,32},{1,65},{17,49},{33,8... | collective-permute-start | bytes 294920 | tf_op jit(solution)/shard_map/ppermute | solution.py:64

commit v5 on v4

--- a/solution.py
+++ b/solution.py
@@ -29,11 +29,14 @@
     there = lax.dynamic_index_in_dim(part, 1 - here, 3, False)
     there = jnp.stack([there[:, :, :, z] for z in PARTNER], axis=3)
     part = lax.dynamic_index_in_dim(part, here, 3, False)
-    part = jnp.where(lax.axis_index("core") == 0, part, there)
-    part = jnp.stack([part[:, :, :, z] for z in NEAR_ORDER[:zb]], axis=3)
-    names = ("y2", "y1", "y0", "zb")
-    part = part.transpose(3, 5, *[names.index(a) for a in ALONG], 4).reshape(zb, 1, own, ys * rows)
-    part = jnp.broadcast_to(part, (zb, yb, own, ys * rows))
+    part = lax.dynamic_index_in_dim(part, lax.axis_index("core"), 1, False)
+    packed = []
+    there = there.swapaxes(0, 1)
+    for rows_of in (there.reshape(ys, zb, rows, own), part.reshape(ys // 2, zb, rows, own)):
+        rows_of = jnp.stack([rows_of[:, z] for z in NEAR_ORDER[:zb]])
+        packed.append(rows_of.transpose(0, 3, 1, 2).reshape(zb, 1, own, -1))
+    part = jnp.concatenate(packed, axis=3)
+    part = jnp.broadcast_to(part, (zb, yb, own, part.shape[3]))
     both = jnp.concatenate([scaled, part], axis=3)
     if NEAR[0] == "y0":
         both = both.transpose(1, 0, 2, 3)
@@ -43,11 +46,12 @@
     )
     both = both.reshape(zb * yb * own, -1)
     factors = both[:, :half]
-    part = lax.all_gather(both[:, half:], "core")
+    split = half + ys * rows
 
-    def product(side):
+    def product(part):
         out = lax.dot_general(
-            part[side], factors, (((0,), (0,)), ((), ())), preferred_element_type=jnp.float32
+            part, factors, (((part.ndim - 2,), (0,)), ((), ())),
+            preferred_element_type=jnp.float32,
         )
         return out.astype(jnp.bfloat16).reshape(ys, rows, half)
 
@@ -58,7 +62,8 @@
         return jnp.sum(block, axis=tuple(i for i in range(3) if i != where))
 
     pairs = [(z, zb + PARTNER[z]) for z in range(zb)] + [(zb + PARTNER[z], z) for z in range(zb)]
-    far, near = product(1), product(0)
+    far, near = lax.optimization_barrier((product(both[:, half:split]), both[:, split:]))
+    near = product(lax.all_gather(near, "core"))
     far = reduce_y(far).astype(jnp.bfloat16)
     far, near = lax.optimization_barrier((far, near))
     far = lax.ppermute(far, ("za", "zb"), pairs)

time: 69.4 us -> 68.3 us (0.984)
  waiting for transfers between devices: 15.3 us -> 9.13 us
  blocking collectives: 26.6 us -> 30.1 us
  other arithmetic: 1.18 us -> 2.96 us
  local copies, waits for them, and re-layouts: 2.55 us -> 1.15 us
  starting transfers between devices: 20.7 us -> 21.5 us
    all_to_all x2, waiting for transfers between devices: 12.8 us -> 6.52 us  [reduce_y(): lax.all_to_all(block, ALONG, split_axis=0, concat_axis=0, tiled=True)]
    all_to_all x1, blocking collectives: 24.2 us -> 27.9 us  [body(): lax.all_to_all(both, NEAR, split_axis=0, concat_axis=0, tiled=True, axis_...]
    unnamed x7 -> x6, local copies, waits for them, and re-layouts: 2.09 us -> 0.5 us
    convert_element_type x1, other arithmetic: 0.1 us -> 1.02 us  [body(): (shaped[:, None] * col_factors.astype(jnp.float32)).astype(jnp.bfloat16)]
    sub x1, other arithmetic: 0.01 us -> 0.71 us  [body(): shaped = fitness_ranks.astype(jnp.float32) / (members - 1) - 0.5]
  transfers between devices with their start and end apart: 3 -> 3, of which waited for: 3 -> 2; matrix products, arithmetic and copies ran while one was open for 2% -> 2% of each run, Pallas kernels for 0% -> 0%
where the time goes in v5:
time: 68.3 us; the launch traced here: 67.5 us
  blocking collectives  30.1 us (44%)
  starting transfers between devices  21.5 us (31%)
  waiting for transfers between devices  9.13 us (13%)
  other arithmetic  2.96 us (4%)
  matrix products  2.48 us (4%)
  local copies, waits for them, and re-layouts  1.15 us (2%)
    all_to_all x1, blocking collectives, body(): lax.all_to_all(both, NEAR, split_axis=0, concat_axis=0, tiled=True, axis_...  27.9 us
    all_to_all x2, starting transfers between devices, reduce_y(): lax.all_to_all(block, ALONG, split_axis=0, concat_axis=0, tiled=True)  10.9 us
    ppermute x1, starting transfers between devices, body(): far = lax.ppermute(far, ('za', 'zb'), pairs)  10.6 us
    all_to_all x2, waiting for transfers between devices, reduce_y(): lax.all_to_all(block, ALONG, split_axis=0, concat_axis=0, tiled=True)  6.52 us
    ppermute x1, waiting for transfers between devices, body(): far = lax.ppermute(far, ('za', 'zb'), pairs)  2.61 us
    dot_general x2, matrix products, product(): lax.dot_general(part, factors, (((part.ndim - 2,), (0,)), ((), ())), pref...  2.48 us
    all_gather x1, blocking collectives, body(): near = product(lax.all_gather(near, 'core'))  2.16 us
  transfers between devices with their start and end apart: 3, of which 2 were waited for; matrix products, arithmetic and copies ran while one was open for 2% of the time, Pallas kernels for 0%

profile of v5, /device:TPU:6, one launch (start us, length us, event | category | flops | bytes accessed | tf_op | source)
XLA Modules:
  0.0 67.5 jit_solution(6451564202354545616)
XLA Ops:
  0.0 0.0 copy-start
  0.0 0.7 %multiply_add_fusion = f32[96]{0:T(128)S(1)} fusion(s32[96]{0:T(128)} %param.7), kind=kLoop, calls=%fused_computation.22 | loop fusion | flops 288 | bytes 768 | tf_op jit(solution)/shard_map/sub | solution.py:23
  0.7 1.0 %multiply_convert_fusion = bf16[96,1024]{1,0:T(8,128)(2,1)S(1)} fusion(bf16[96,1024]{1,0:T(8,128)(2,1)} %param.6, f32[96]{0:T(128)S(1)} %multiply_add_fusion), kind=kLoop, calls=%fused_computation.9 | loop fusion | flops 294912 | bytes 393600 | tf_op jit(solution)/shard_map/convert_element_type | solution.py:24
  1.7 0.1 reshape.49
  1.9 0.0 copy-done
  1.9 0.3 copy.32
  2.3 0.1 maximum_bitcast_fusion.1
  2.5 0.1 pad_maximum_fusion.1
  2.6 0.1 maximum_bitcast_fusion
  2.7 0.2 copy.37
  3.0 0.1 broadcast_in_dim.13
  3.1 0.1 pad_maximum_fusion
  3.2 27.9 %all_to_all.15 = bf16[6,96,1088]{2,1,0:T(8,128)(2,1)S(1)} all-to-all(bf16[6,96,1088]{2,1,0:T(8,128)(2,1)S(1)} %bitcast.52), channel_id=1, replica_groups={{16,32,0,112,128,96},{17,33,1,113,129,97},{18,34,2,114,130,98},{19,35,3..., dimensions={0} | all-to-all | bytes 2506752 | tf_op jit(solution)/shard_map/all_to_all | solution.py:44
  31.1 1.3 %convolution_convert_fusion.1 = bf16[384,512]{1,0:T(8,128)(2,1)} fusion(bf16[576,1088]{1,0:T(8,128)(2,1)S(1)} %bitcast.54), kind=kOutput, calls=%fused_computation.2 | convolution fusion | flops 226689024 | bytes 1425408 | tf_op jit(solution)/shard_map/dot_general | solution.py:52
  32.4 6.2 %all-to-all-start.1 = ((bf16[8,48,512]{2,1,0:T(8,128)(2,1)}), bf16[8,48,512]{2,1,0:T(8,128)(2,1)S(1)}, u32[]{:S(2)}, u32[]{:S(2)}) async-start(bf16[8,48,512]{2,1,0:T(8,128)(2,1)} %bitcast.20), calls=%async_computation.1 | async-start | bytes 786432 | tf_op jit(solution)/shard_map/all_to_all | solution.py:59
  38.6 0.2 copy.38
  38.8 2.2 %all-gather.1 = bf16[2,576,192]{1,2,0:T(8,128)(2,1)S(1)} all-gather(bf16[1,576,192]{1,2,0:T(8,128)(2,1)S(1)} %copy.38), channel_id=2, replica_groups=mesh['y2'=2,'y1'=2,'y0'=2,'za'=2,'zb'=3,'plane'=8,'core'=2] {'core'}, dimensions={0}, use_global_device_ids=true | all-gather | bytes 663552 | tf_op jit(solution)/shard_map/all_gather | solution.py:66
  40.9 1.2 %convolution_convert_fusion = bf16[2,192,512]{2,1,0:T(8,128)(2,1)} fusion(bf16[2,576,192]{1,2,0:T(8,128)(2,1)S(1)} %all-gather.1, bf16[576,1088]{1,0:T(8,128)(2,1)S(1)} %bitcast.55), kind=kOutput, calls=%fused_computation.1 | convolution fusion | flops 226689024 | bytes 1474560 | tf_op jit(solution)/shard_map/dot_general | solution.py:52
  42.1 6.5 %all-to-all-done.1 = bf16[8,48,512]{2,1,0:T(8,128)(2,1)S(1)} async-done(((bf16[8,48,512]{2,1,0:T(8,128)(2,1)}), bf16[8,48,512]{2,1,0:T(8,128)(2,1)S(1)}, u32[]{:S(2)}, u32[]{:S(2)}) %all-to-all-start.1) | async-done | bytes 393248 | tf_op jit(solution)/shard_map/all_to_all | solution.py:59
  48.7 0.0 copy-start.1
  48.7 0.1 reduce
  48.7 4.7 %all-to-all-start.2 = ((bf16[8,48,512]{2,1,0:T(8,128)(2,1)}), bf16[8,48,512]{2,1,0:T(8,128)(2,1)S(1)}, u32[]{:S(2)}, u32[]{:S(2)}) async-start(bf16[8,48,512]{2,1,0:T(8,128)(2,1)} %bitcast.24), calls=%async_computation.2 | async-start | bytes 786432 | tf_op jit(solution)/shard_map/all_to_all | solution.py:59
  53.4 10.6 %collective-permute-start = (bf16[2,48,512]{2,1,0:T(8,128)(2,1)S(1)}, bf16[2,48,512]{2,1,0:T(8,128)(2,1)S(1)}, u32[]{:S(2)}, u32[]{:S(2)}) collective-permute-start(bf16[2,48,512]{2,1,0:T(8,128)(2,1)S(1)} %reduce), channel_id=1, source_target_pairs={{0,64},{16,48},{32,80},{64,0},{48,16},{80,32},{1,65},{17,49},{33,8... | collective-permute-start | bytes 294920 | tf_op jit(solution)/shard_map/ppermute | solution.py:69
  64.0 0.0 all-to-all-done.2
  64.0 0.1 convert_reduce_fusion
  64.1 2.6 %collective-permute-done = bf16[2,48,512]{2,1,0:T(8,128)(2,1)S(1)} collective-permute-done((bf16[2,48,512]{2,1,0:T(8,128)(2,1)S(1)}, bf16[2,48,512]{2,1,0:T(8,128)(2,1)S(1)}, u32[]{:S(2)}, u32[]{:S(2)}) %collective-permute-start) | collective-permute-done | bytes 98336 | tf_op jit(solution)/shard_map/ppermute | solution.py:69
  66.8 0.0 copy-done.1
  66.8 0.7 %add.30 = f32[48,1024]{1,0:T(8,128)} add(f32[48,1024]{1,0:T(8,128)S(1)} %copy-done.1, f32[48,1024]{1,0:T(8,128)S(1)} %bitcast.64) | non-fusion elementwise | flops 49152 | bytes 589824 | tf_op jit(solution)/shard_map/add | solution.py:72
  (12 shorter events, 0.3 us)
Async XLA Ops:
  0.0 1.9 %copy-start = (bf16[2304,96]{0,1:T(8,128)(2,1)S(1)}, bf16[2304,96]{0,1:T(8,128)(2,1)}, u32[]{:S(2)}) copy-start(bf16[2304,96]{0,1:T(8,128)(2,1)} %param.5) | copy-start | bytes 1327108
  32.4 16.3 %all-to-all-start.1 = ((bf16[8,48,512]{2,1,0:T(8,128)(2,1)}), bf16[8,48,512]{2,1,0:T(8,128)(2,1)S(1)}, u32[]{:S(2)}, u32[]{:S(2)}) async-start(bf16[8,48,512]{2,1,0:T(8,128)(2,1)} %bitcast.20), calls=%async_computation.1 | async-start | bytes 786432 | tf_op jit(solution)/shard_map/all_to_all | solution.py:59
  48.7 18.1 %copy-start.1 = (f32[48,1024]{1,0:T(8,128)S(1)}, f32[48,1024]{1,0:T(8,128)}, u32[]{:S(2)}) copy-start(f32[48,1024]{1,0:T(8,128)} %param.4) | copy-start | bytes 589828
  48.7 15.3 %all-to-all-start.2 = ((bf16[8,48,512]{2,1,0:T(8,128)(2,1)}), bf16[8,48,512]{2,1,0:T(8,128)(2,1)S(1)}, u32[]{:S(2)}, u32[]{:S(2)}) async-start(bf16[8,48,512]{2,1,0:T(8,128)(2,1)} %bitcast.24), calls=%async_computation.2 | async-start | bytes 786432 | tf_op jit(solution)/shard_map/all_to_all | solution.py:59
  53.4 13.3 %collective-permute-start = (bf16[2,48,512]{2,1,0:T(8,128)(2,1)S(1)}, bf16[2,48,512]{2,1,0:T(8,128)(2,1)S(1)}, u32[]{:S(2)}, u32[]{:S(2)}) collective-permute-start(bf16[2,48,512]{2,1,0:T(8,128)(2,1)S(1)} %reduce), channel_id=1, source_target_pairs={{0,64},{16,48},{32,80},{64,0},{48,16},{80,32},{1,65},{17,49},{33,8... | collective-permute-start | bytes 294920 | tf_op jit(solution)/shard_map/ppermute | solution.py:69

commit v6 on v5

--- a/solution.py
+++ b/solution.py
@@ -8,7 +8,7 @@
 YB, ZB = 2, 3
 NEAR = ("y0", "zb")
 NEAR_ORDER = (1, 2, 0, 4, 5, 3)
-PARTNER = (1, 0, 2)
+PARTNER = (0, 1, 2)
 ALONG = ("y1", "y2", "y0")
 
 
@@ -61,13 +61,14 @@
         where = ALONG.index("y0")
         return jnp.sum(block, axis=tuple(i for i in range(3) if i != where))
 
-    pairs = [(z, zb + PARTNER[z]) for z in range(zb)] + [(zb + PARTNER[z], z) for z in range(zb)]
+    back = [(zb + PARTNER[z], z) for z in range(zb)]
     far, near = lax.optimization_barrier((product(both[:, half:split]), both[:, split:]))
     near = product(lax.all_gather(near, "core"))
     far = reduce_y(far).astype(jnp.bfloat16)
+    first = lax.ppermute(far, ("za", "zb"), back)
     far, near = lax.optimization_barrier((far, near))
-    far = lax.ppermute(far, ("za", "zb"), pairs)
-    update = reduce_y(near) + far.astype(jnp.float32)
+    second = lax.ppermute(far, ("za", "zb"), [(b, a) for a, b in back])
+    update = reduce_y(near) + (first.astype(jnp.float32) + second.astype(jnp.float32))
     update = update.transpose(1, 0, 2).reshape(rows, cols)
     return weight + 3.0 / math.sqrt(members) * update
 

time: 68.3 us -> 68.4 us (level)
    ppermute x1 -> x2, starting transfers between devices: 10.6 us -> 10.3 us  [the longest x1 9.06 us: body(): second = lax.ppermute(far, ('za', 'zb'), [(b, a) for a, b in back])]
    ppermute x1 -> x2, waiting for transfers between devices: 2.61 us -> 2.61 us  [the longest x1 2.61 us: body(): first = lax.ppermute(far, ('za', 'zb'), back)]
  transfers between devices with their start and end apart: 3 -> 4, of which waited for: 2 -> 2; matrix products, arithmetic and copies ran while one was open for 2% -> 2% of each run, Pallas kernels for 0% -> 0%
where the time goes in v6:
time: 68.4 us; the launch traced here: 67.1 us
  blocking collectives  30.1 us (44%)
  starting transfers between devices  21.2 us (31%)
  waiting for transfers between devices  9.13 us (13%)
  other arithmetic  2.91 us (4%)
  matrix products  2.47 us (4%)
  local copies, waits for them, and re-layouts  1.13 us (2%)
    all_to_all x1, blocking collectives, body(): lax.all_to_all(both, NEAR, split_axis=0, concat_axis=0, tiled=True, axis_...  27.9 us
    all_to_all x2, starting transfers between devices, reduce_y(): lax.all_to_all(block, ALONG, split_axis=0, concat_axis=0, tiled=True)  10.9 us
    ppermute x1, starting transfers between devices, body(): second = lax.ppermute(far, ('za', 'zb'), [(b, a) for a, b in back])  9.06 us
    all_to_all x2, waiting for transfers between devices, reduce_y(): lax.all_to_all(block, ALONG, split_axis=0, concat_axis=0, tiled=True)  6.52 us
    ppermute x1, waiting for transfers between devices, body(): first = lax.ppermute(far, ('za', 'zb'), back)  2.61 us
    dot_general x2, matrix products, product(): lax.dot_general(part, factors, (((part.ndim - 2,), (0,)), ((), ())), pref...  2.47 us
    all_gather x1, blocking collectives, body(): near = product(lax.all_gather(near, 'core'))  2.16 us
  transfers between devices with their start and end apart: 4, of which 2 were waited for; matrix products, arithmetic and copies ran while one was open for 2% of the time, Pallas kernels for 0%

profile of v6, /device:TPU:6, one launch (start us, length us, event | category | flops | bytes accessed | tf_op | source)
XLA Modules:
  0.0 67.1 jit_solution(9168656132228317281)
XLA Ops:
  0.0 0.0 copy-start
  0.0 0.7 %multiply_add_fusion = f32[96]{0:T(128)S(1)} fusion(s32[96]{0:T(128)} %param.7), kind=kLoop, calls=%fused_computation.21 | loop fusion | flops 288 | bytes 768 | tf_op jit(solution)/shard_map/sub | solution.py:23
  0.7 1.0 %multiply_convert_fusion = bf16[96,1024]{1,0:T(8,128)(2,1)S(1)} fusion(bf16[96,1024]{1,0:T(8,128)(2,1)} %param.6, f32[96]{0:T(128)S(1)} %multiply_add_fusion), kind=kLoop, calls=%fused_computation.9 | loop fusion | flops 294912 | bytes 393600 | tf_op jit(solution)/shard_map/convert_element_type | solution.py:24
  1.7 0.1 reshape.49
  1.9 0.0 copy-done
  1.9 0.3 copy.32
  2.4 0.1 pad_maximum_fusion.1
  2.5 0.1 maximum_bitcast_fusion
  2.6 0.2 copy.37
  2.9 0.1 broadcast_in_dim.13
  3.0 0.1 pad_maximum_fusion
  3.1 27.9 %all_to_all.15 = bf16[6,96,1088]{2,1,0:T(8,128)(2,1)S(1)} all-to-all(bf16[6,96,1088]{2,1,0:T(8,128)(2,1)S(1)} %bitcast.52), channel_id=1, replica_groups={{16,32,0,112,128,96},{17,33,1,113,129,97},{18,34,2,114,130,98},{19,35,3..., dimensions={0} | all-to-all | bytes 2506752 | tf_op jit(solution)/shard_map/all_to_all | solution.py:44
  31.0 1.3 %convolution_convert_fusion.1 = bf16[384,512]{1,0:T(8,128)(2,1)} fusion(bf16[576,1088]{1,0:T(8,128)(2,1)S(1)} %bitcast.54), kind=kOutput, calls=%fused_computation.2 | convolution fusion | flops 226689024 | bytes 1425408 | tf_op jit(solution)/shard_map/dot_general | solution.py:52
  32.3 6.2 %all-to-all-start.1 = ((bf16[8,48,512]{2,1,0:T(8,128)(2,1)}), bf16[8,48,512]{2,1,0:T(8,128)(2,1)S(1)}, u32[]{:S(2)}, u32[]{:S(2)}) async-start(bf16[8,48,512]{2,1,0:T(8,128)(2,1)} %bitcast.20), calls=%async_computation.1 | async-start | bytes 786432 | tf_op jit(solution)/shard_map/all_to_all | solution.py:59
  38.5 0.2 copy.38
  38.7 2.2 %all-gather.1 = bf16[2,576,192]{1,2,0:T(8,128)(2,1)S(1)} all-gather(bf16[1,576,192]{1,2,0:T(8,128)(2,1)S(1)} %copy.38), channel_id=2, replica_groups=mesh['y2'=2,'y1'=2,'y0'=2,'za'=2,'zb'=3,'plane'=8,'core'=2] {'core'}, dimensions={0}, use_global_device_ids=true | all-gather | bytes 663552 | tf_op jit(solution)/shard_map/all_gather | solution.py:66
  40.8 1.2 %convolution_convert_fusion = bf16[2,192,512]{2,1,0:T(8,128)(2,1)} fusion(bf16[2,576,192]{1,2,0:T(8,128)(2,1)S(1)} %all-gather.1, bf16[576,1088]{1,0:T(8,128)(2,1)S(1)} %bitcast.55), kind=kOutput, calls=%fused_computation.1 | convolution fusion | flops 226689024 | bytes 1474560 | tf_op jit(solution)/shard_map/dot_general | solution.py:52
  42.0 6.5 %all-to-all-done.1 = bf16[8,48,512]{2,1,0:T(8,128)(2,1)S(1)} async-done(((bf16[8,48,512]{2,1,0:T(8,128)(2,1)}), bf16[8,48,512]{2,1,0:T(8,128)(2,1)S(1)}, u32[]{:S(2)}, u32[]{:S(2)}) %all-to-all-start.1) | async-done | bytes 393248 | tf_op jit(solution)/shard_map/all_to_all | solution.py:59
  48.6 0.0 copy-start.1
  48.6 0.1 reduce
  48.6 4.7 %all-to-all-start.2 = ((bf16[8,48,512]{2,1,0:T(8,128)(2,1)}), bf16[8,48,512]{2,1,0:T(8,128)(2,1)S(1)}, u32[]{:S(2)}, u32[]{:S(2)}) async-start(bf16[8,48,512]{2,1,0:T(8,128)(2,1)} %bitcast.24), calls=%async_computation.2 | async-start | bytes 786432 | tf_op jit(solution)/shard_map/all_to_all | solution.py:59
  53.3 1.3 %collective-permute-start = (bf16[2,48,512]{2,1,0:T(8,128)(2,1)S(1)}, bf16[2,48,512]{2,1,0:T(8,128)(2,1)S(1)}, u32[]{:S(2)}, u32[]{:S(2)}) collective-permute-start(bf16[2,48,512]{2,1,0:T(8,128)(2,1)S(1)} %reduce), channel_id=1, source_target_pairs={{48,0},{64,16},{80,32},{49,1},{65,17},{81,33},{50,2},{66,18},{82,3... | collective-permute-start | bytes 294920 | tf_op jit(solution)/shard_map/ppermute | solution.py:68
  54.6 9.1 %collective-permute-start.1 = (bf16[2,48,512]{2,1,0:T(8,128)(2,1)S(1)}, bf16[2,48,512]{2,1,0:T(8,128)(2,1)S(1)}, u32[]{:S(2)}, u32[]{:S(2)}) collective-permute-start(bf16[2,48,512]{2,1,0:T(8,128)(2,1)S(1)} %reduce), channel_id=1, source_target_pairs={{0,48},{16,64},{32,80},{1,49},{17,65},{33,81},{2,50},{18,66},{34,8... | collective-permute-start | bytes 294920 | tf_op jit(solution)/shard_map/ppermute | solution.py:70
  63.7 0.0 all-to-all-done.2
  63.7 0.1 convert_reduce_fusion
  63.7 2.6 %collective-permute-done = bf16[2,48,512]{2,1,0:T(8,128)(2,1)S(1)} collective-permute-done((bf16[2,48,512]{2,1,0:T(8,128)(2,1)S(1)}, bf16[2,48,512]{2,1,0:T(8,128)(2,1)S(1)}, u32[]{:S(2)}, u32[]{:S(2)}) %collective-permute-start) | collective-permute-done | bytes 98336 | tf_op jit(solution)/shard_map/ppermute | solution.py:68
  66.3 0.0 collective-permute-done.1
  66.4 0.0 copy-done.1
  66.4 0.7 %add.34 = f32[48,1024]{1,0:T(8,128)} add(f32[48,1024]{1,0:T(8,128)S(1)} %copy-done.1, f32[48,1024]{1,0:T(8,128)S(1)} %bitcast.64) | non-fusion elementwise | flops 49152 | bytes 589824 | tf_op jit(solution)/shard_map/add | solution.py:73
  (11 shorter events, 0.3 us)
Async XLA Ops:
  0.0 1.9 %copy-start = (bf16[2304,96]{0,1:T(8,128)(2,1)S(1)}, bf16[2304,96]{0,1:T(8,128)(2,1)}, u32[]{:S(2)}) copy-start(bf16[2304,96]{0,1:T(8,128)(2,1)} %param.5) | copy-start | bytes 1327108
  32.3 16.3 %all-to-all-start.1 = ((bf16[8,48,512]{2,1,0:T(8,128)(2,1)}), bf16[8,48,512]{2,1,0:T(8,128)(2,1)S(1)}, u32[]{:S(2)}, u32[]{:S(2)}) async-start(bf16[8,48,512]{2,1,0:T(8,128)(2,1)} %bitcast.20), calls=%async_computation.1 | async-start | bytes 786432 | tf_op jit(solution)/shard_map/all_to_all | solution.py:59
  48.6 17.9 %copy-start.1 = (f32[48,1024]{1,0:T(8,128)S(1)}, f32[48,1024]{1,0:T(8,128)}, u32[]{:S(2)}) copy-start(f32[48,1024]{1,0:T(8,128)} %param.4) | copy-start | bytes 589828
  48.6 15.1 %all-to-all-start.2 = ((bf16[8,48,512]{2,1,0:T(8,128)(2,1)}), bf16[8,48,512]{2,1,0:T(8,128)(2,1)S(1)}, u32[]{:S(2)}, u32[]{:S(2)}) async-start(bf16[8,48,512]{2,1,0:T(8,128)(2,1)} %bitcast.24), calls=%async_computation.2 | async-start | bytes 786432 | tf_op jit(solution)/shard_map/all_to_all | solution.py:59
  53.3 13.0 %collective-permute-start = (bf16[2,48,512]{2,1,0:T(8,128)(2,1)S(1)}, bf16[2,48,512]{2,1,0:T(8,128)(2,1)S(1)}, u32[]{:S(2)}, u32[]{:S(2)}) collective-permute-start(bf16[2,48,512]{2,1,0:T(8,128)(2,1)S(1)} %reduce), channel_id=1, source_target_pairs={{48,0},{64,16},{80,32},{49,1},{65,17},{81,33},{50,2},{66,18},{82,3... | collective-permute-start | bytes 294920 | tf_op jit(solution)/shard_map/ppermute | solution.py:68
  54.6 11.7 %collective-permute-start.1 = (bf16[2,48,512]{2,1,0:T(8,128)(2,1)S(1)}, bf16[2,48,512]{2,1,0:T(8,128)(2,1)S(1)}, u32[]{:S(2)}, u32[]{:S(2)}) collective-permute-start(bf16[2,48,512]{2,1,0:T(8,128)(2,1)S(1)} %reduce), channel_id=1, source_target_pairs={{0,48},{16,64},{32,80},{1,49},{17,65},{33,81},{2,50},{18,66},{34,8... | collective-permute-start | bytes 294920 | tf_op jit(solution)/shard_map/ppermute | solution.py:70
